TPU v7x, 32 devices: a whole 2x2x4 slice. The times are simulated.
32 devices in a mesh: surf: 8 (over z, x), rad: 4 (over y, core).
Axes of the slice: x: 2, y: 2, z: 4, core: 2. Of those that a mesh axis runs over, the one named last changes fastest.
Arguments:
- displacement: float32 [3, 128, 32, 512], P(None, 'surf', 'rad'), may hold values from -6 to 6
- velocity: float32 [3, 128, 32, 512], P(None, 'surf', 'rad'), may hold values from -6 to 6
- source: float32 [3, 128, 32, 512], P(None, 'surf', 'rad'), may hold values from -6 to 6
- lame_first: float32 [128, 32, 512], P('surf', 'rad'), may hold values from 0.5 to 2
- shear_modulus: float32 [128, 32, 512], P('surf', 'rad'), may hold values from 0.5 to 2
- density: float32 [128, 32, 512], P('surf', 'rad'), may hold values from 1 to 3
- shell_kappa: float32 [32, 4, 128], P('surf'), may hold values from 0.5 to 4
Outputs:
- displacement_next: float32 [3, 128, 32, 512], P(None, 'surf', 'rad')
- velocity_next: float32 [3, 128, 32, 512], P(None, 'surf', 'rad')
- potential: float32 [32, 8, 128], P('surf', 'rad')
All inputs are finite; a program needn't handle non-finite values.
Results may differ from a plain program's by a relative error of at most 0.0003.
Values sent between devices are 32-bit elements; how exact they have to be, the bound alone decides.
A program may use at most 128 MiB of HBM per device.

v0:
```python
import functools

import jax
import jax.numpy as jnp
import numpy as np
from jax import lax
from jax.experimental import pallas as pl
from jax.experimental.pallas import tpu as pltpu
from jax.sharding import PartitionSpec as P

CYCLES = 2
STEPS = 3

time_step = 0.005
coupling = 4.0
upper_margin = 1.1
spectrum_ratio = 10.0
MESH = pl.DeviceIdType.MESH
VMEM = pl.BlockSpec(memory_space=pltpu.VMEM)
SMEM = pl.BlockSpec(memory_space=pltpu.SMEM)
LIMIT = 48 * 1024 * 1024


def node_tables():
    points = np.array([-1.0, -np.sqrt(3.0 / 7.0), 0.0, np.sqrt(3.0 / 7.0), 1.0])
    weights = np.array([0.1, 49.0 / 90.0, 32.0 / 45.0, 49.0 / 90.0, 0.1])
    scales = np.array(
        [
            np.prod([points[outer] - points[inner] for inner in range(5) if inner != outer])
            for outer in range(5)
        ]
    )
    derivative = np.zeros((5, 5))
    for row_index in range(5):
        for col_index in range(5):
            if row_index != col_index:
                derivative[row_index, col_index] = (
                    scales[row_index] / scales[col_index] / (points[row_index] - points[col_index])
                )
            else:
                derivative[row_index, col_index] = sum(
                    (
                        1.0 / (points[col_index] - points[inner])
                        for inner in range(5)
                        if inner != col_index
                    )
                )
    return (derivative, weights)


DERIVATIVE, WEIGHTS = node_tables()


def line_product(matrix, u):
    u0, u1, u2, u3, u4 = u
    s0, d0, s1, d1 = u0 + u4, u0 - u4, u1 + u3, u1 - u3

    def scaled(terms):
        total = None
        for factor, value in terms:
            if abs(factor) < 1e-12:
                continue
            term = value * np.float32(factor)
            total = term if total is None else total + term
        return total

    even = [
        scaled(
            [
                (0.5 * (matrix[p, 0] + matrix[p, 4]), s0),
                (0.5 * (matrix[p, 1] + matrix[p, 3]), s1),
                (matrix[p, 2], u2),
            ]
        )
        for p in range(2)
    ]
    odd = [
        scaled(
            [
                (0.5 * (matrix[p, 0] - matrix[p, 4]), d0),
                (0.5 * (matrix[p, 1] - matrix[p, 3]), d1),
            ]
        )
        for p in range(3)
    ]
    return [even[0] + odd[0], even[1] + odd[1], odd[2], odd[1] - even[1], odd[0] - even[0]]


def three_parts(values):
    high = values.astype(jnp.bfloat16)
    rest = values - high.astype(jnp.float32)
    middle = rest.astype(jnp.bfloat16)
    low = (rest - middle.astype(jnp.float32)).astype(jnp.bfloat16)
    return high, middle, low


def dot(first, second):
    return jnp.dot(first, second, preferred_element_type=jnp.float32)


def row_tables(nodes_x, nodes_z):
    own = nodes_x * nodes_z
    elem_x, elem_z = nodes_x // 4, nodes_z // 4
    tile = elem_x * elem_z
    rows = own + nodes_z + nodes_x + 8
    points = -(-25 * tile // 16) * 16
    pick = np.zeros((points, rows), np.float32)
    for a in range(5):
        for b in range(5):
            for f in range(elem_z):
                for e in range(elem_x):
                    x, z = 4 * e + a, 4 * f + b
                    if x < nodes_x and z < nodes_z:
                        row = x * nodes_z + z
                    elif z < nodes_z:
                        row = own + z
                    elif x < nodes_x:
                        row = own + nodes_z + x
                    else:
                        row = own + nodes_z + nodes_x
                    pick[(a * 5 + b) * tile + f * elem_x + e, row] = 1.0
    return pick


def lane_tables(nodes_y):
    elem_y = nodes_y // 4
    fold = np.zeros((5 * elem_y, nodes_y), np.float32)
    for c in range(5):
        for g in range(elem_y):
            fold[c * elem_y + g, (4 * g + c) % nodes_y] = 1.0
    return fold


def halo_kernel(surf, rad, disp, lame, shear, dense, plane, level, send, recv, send_sem, recv_sem):
    s, r = lax.axis_index("surf"), lax.axis_index("rad")
    nodes_x, nodes_z = disp.shape[1], disp.shape[2]
    s_low, s_high = lax.rem(s + surf - 1, surf), lax.rem(s + 1, surf)
    r_low, r_high = lax.rem(r + rad - 1, rad), lax.rem(r + 1, rad)
    barrier = pltpu.get_barrier_semaphore()
    for target in ((s_high, r), (s, r_high), (s_high, r_high)):
        pl.semaphore_signal(barrier, inc=1, device_id=target, device_id_type=MESH)
    for i in range(6):
        ref = disp.at[i] if i < 3 else (lame, shear, dense)[i - 3]
        send[i, 0:nodes_z, :] = ref[0]
        for x in range(nodes_x):
            send[i, nodes_z + x : nodes_z + x + 1, :] = ref[x, 0:1, :]
        send[i, nodes_z + nodes_x :, :] = ref[0]
    pl.semaphore_wait(barrier, 3)
    pieces = (
        (0, nodes_z, (s_low, r)),
        (nodes_z, nodes_x, (s, r_low)),
        (nodes_z + nodes_x, 8, (s_low, r_low)),
    )
    copies = []
    for k, (start, size, target) in enumerate(pieces):
        copy = pltpu.make_async_remote_copy(
            src_ref=send.at[:, pl.ds(start, size)],
            dst_ref=recv.at[:, pl.ds(start, size)],
            send_sem=send_sem.at[k],
            recv_sem=recv_sem.at[k],
            device_id=target,
            device_id_type=MESH,
        )
        copy.start()
        copies.append(copy)
    for copy in copies:
        copy.wait()
    plane[...] = recv[:, 0:nodes_z, :]
    level[...] = jnp.where(r == rad - 1, 0.0, recv[:, nodes_z:, :])


def element_kernel(
    elem_x,
    elem_z,
    disp,
    lame,
    shear,
    dense,
    kappa,
    plane,
    level,
    unfold,
    fold,
    pick,
    gather,
    weight,
    own_out,
    plane_out,
    level_out,
    payload,
    views,
    grads,
    terms,
    force,
):
    own, nodes_y = lame.shape
    elem_y = nodes_y // 4
    tile = elem_x * elem_z
    points = pick.shape[0]
    r = lax.axis_index("rad")

    def at(i, c):
        return i, slice(c * elem_y, (c + 1) * elem_y)

    for i in range(6):
        ref = disp.at[i] if i < 3 else (lame, shear, dense)[i - 3]
        extended = jnp.concatenate([ref[...], plane[i], level[i]], axis=0)
        lanes = sum(dot(part, unfold[...]) for part in three_parts(extended))
        stacked = jnp.concatenate(three_parts(lanes), axis=0)
        picked = dot(gather[...], stacked)
        views[i, :, :nodes_y] = picked
        views[i, :, nodes_y:] = pltpu.roll(picked[:, :elem_y], elem_y - 1, 1)

    def rows(a, b):
        return pl.ds(pl.multiple_of((a * 5 + b) * tile, tile), tile)

    def lanes_of(c):
        return pl.ds(c * elem_y, elem_y)

    def x_gradients(b, carry):
        for c in range(5):
            for i in range(3):
                line = [views[i, rows(a, b), lanes_of(c)] for a in range(5)]
                for a, value in enumerate(line_product(DERIVATIVE, line)):
                    grads[i, rows(a, b), lanes_of(c)] = value
        return carry

    lax.fori_loop(0, 5, x_gradients, 0)

    def z_gradients(a, carry):
        for c in range(5):
            for i in range(3):
                line = [views[i, rows(a, b), lanes_of(c)] for b in range(5)]
                for b, value in enumerate(line_product(DERIVATIVE, line)):
                    grads[3 + i, rows(a, b), lanes_of(c)] = value
        return carry

    lax.fori_loop(0, 5, z_gradients, 0)

    def stresses(a, total):
        for b in range(5):
            here = rows(a, b)
            along = [
                line_product(DERIVATIVE, [views[i, here, lanes_of(c)] for c in range(5)])
                for i in range(3)
            ]
            toward = [[], [], []]
            for c in range(5):
                scale = weight[a * 25 + b * 5 + c]
                mu = views[4, here, lanes_of(c)] * scale
                x0, x1, x2 = [grads[i, here, lanes_of(c)] for i in range(3)]
                z0, z1, z2 = [grads[3 + i, here, lanes_of(c)] for i in range(3)]
                y0, y1, y2 = [along[i][c] for i in range(3)]
                dilatation = x0 + z1 + y2
                total = total + (views[5, here, lanes_of(c)] * scale) * dilatation
                spread = (views[3, here, lanes_of(c)] * scale) * dilatation
                double = mu + mu
                terms[0, here, lanes_of(c)] = double * x0 + spread
                terms[1, here, lanes_of(c)] = mu * (x1 + z0)
                terms[2, here, lanes_of(c)] = mu * (x2 + y0)
                terms[3, here, lanes_of(c)] = double * z1 + spread
                terms[4, here, lanes_of(c)] = mu * (z2 + y1)
                toward[0].append(mu * (x2 + y0))
                toward[1].append(mu * (z2 + y1))
                toward[2].append(double * y2 + spread)
            for i in range(3):
                for c, value in enumerate(line_product(-DERIVATIVE.T, toward[i])):
                    force[i, here, lanes_of(c)] = value
        return total

    total = lax.fori_loop(0, 5, stresses, jnp.zeros((tile, elem_y), jnp.float32))
    change = -coupling * total
    for f in range(elem_z):
        payload[f] = change[f * elem_x : (f + 1) * elem_x]
    shell = jnp.zeros((elem_x, elem_y), jnp.float32)
    for k in range(kappa.shape[1]):
        level_rows = jnp.concatenate([kappa[e, k : k + 1, :] for e in range(elem_x)], axis=0)
        shell = jnp.where(r == k, level_rows, shell)
    payload[elem_z] = shell

    def z_forces(a, carry):
        for c in range(5):
            for i, term in enumerate((1, 3, 4)):
                line = [terms[term, rows(a, b), lanes_of(c)] for b in range(5)]
                for b, value in enumerate(line_product(-DERIVATIVE.T, line)):
                    force[i, rows(a, b), lanes_of(c)] += value
        return carry

    lax.fori_loop(0, 5, z_forces, 0)

    def x_forces(b, carry):
        for c in range(5):
            for i in range(3):
                line = [terms[i, rows(a, b), lanes_of(c)] for a in range(5)]
                for a, value in enumerate(line_product(-DERIVATIVE.T, line)):
                    force[i, rows(a, b), lanes_of(c)] += value
        return carry

    lax.fori_loop(0, 5, x_forces, 0)
    if points > 25 * tile:
        force[:, 25 * tile :, :] = jnp.zeros((3, points - 25 * tile, 5 * elem_y), jnp.float32)
    nodes_z = plane_out.shape[1]
    for i in range(3):
        merged = sum(dot(pick[...], part) for part in three_parts(force[i]))
        whole = sum(dot(part, fold[...]) for part in three_parts(merged))
        own_out[i] = whole[:own]
        plane_out[i] = whole[own : own + nodes_z]
        level_out[i] = whole[own + nodes_z :]


def exchange_kernel(
    surf, rad, plane, level, payload, plane_in, level_in, cells, force_send, force_recv, send_sem, recv_sem
):
    s, r = lax.axis_index("surf"), lax.axis_index("rad")
    nodes_x = level.shape[1] - 8
    peers = surf * rad
    barrier = pltpu.get_barrier_semaphore()

    def peer_of(k):
        return (lax.rem(s + k // rad, surf), lax.rem(r + lax.rem(k, rad), rad))

    def greet(k, carry):
        pl.semaphore_signal(barrier, inc=1, device_id=peer_of(k), device_id_type=MESH)
        return carry

    lax.fori_loop(1, peers, greet, 0)
    pl.semaphore_wait(barrier, peers - 1)
    s_high, r_high = lax.rem(s + 1, surf), lax.rem(r + 1, rad)
    near = level.at[:, pl.ds(0, nodes_x)], level_in.at[:, pl.ds(0, nodes_x)]
    corner = level.at[:, pl.ds(nodes_x, 8)], level_in.at[:, pl.ds(nodes_x, 8)]
    pieces = (
        (plane, plane_in, (s_high, r)),
        (*near, (s, r_high)),
        (*corner, (s_high, r_high)),
    )

    def cell_copy(k, owner):
        return pltpu.make_async_remote_copy(
            src_ref=payload,
            dst_ref=cells.at[owner, :, lax.rem(surf - k // rad, surf)],
            send_sem=send_sem.at[k],
            recv_sem=recv_sem.at[k],
            device_id=peer_of(k),
            device_id_type=MESH,
        )

    def begin(k, carry):
        cell_copy(k, r).start()
        return carry

    lax.fori_loop(1, peers, begin, 0)
    copies = []
    for k, (source, target, peer) in enumerate(pieces):
        copy = pltpu.make_async_remote_copy(
            src_ref=source,
            dst_ref=target,
            send_sem=force_send.at[k],
            recv_sem=force_recv.at[k],
            device_id=peer,
            device_id_type=MESH,
        )
        copy.start()
        copies.append(copy)
    cells[r, :, 0] = payload[...]

    def finish(k, carry):
        copy = cell_copy(k, lax.rem(r + rad - lax.rem(k, rad), rad))
        copy.wait_send()
        copy.wait_recv()
        return carry

    lax.fori_loop(1, peers, finish, 0)
    for copy in copies:
        copy.wait()


def smooth(forcing, apply_operator):
    def total(values):
        return jnp.sum(jnp.sum(values, axis=0), axis=(0, 1), keepdims=True)[None]

    potential_all = jnp.zeros_like(forcing)
    residual = forcing
    for cycle_index in range(CYCLES):
        applied = apply_operator(residual)
        upper_bound = upper_margin * total(applied * applied) / total(residual * applied)
        lower_bound = upper_bound / spectrum_ratio
        midpoint = 0.5 * (upper_bound + lower_bound)
        half_width = 0.5 * (upper_bound - lower_bound)
        spread = midpoint / half_width
        previous = 1.0 / spread
        inverse = 1.0 / midpoint
        correction = residual * inverse
        potential_all = potential_all + correction
        residual = residual - applied * inverse
        for step_index in range(1, STEPS):
            weighting = 1.0 / (2.0 * spread - previous)
            correction = (weighting * previous) * correction + (
                2.0 * weighting / half_width
            ) * residual
            previous = weighting
            potential_all = potential_all + correction
            if cycle_index < CYCLES - 1 or step_index < STEPS - 1:
                residual = residual - apply_operator(correction)
    return potential_all


def finish_kernel(
    rad,
    disp,
    velocity,
    source,
    dense,
    own_force,
    plane_in,
    level_in,
    cells,
    weight_zy,
    disp_next,
    velocity_next,
    potential,
    held,
):
    r = lax.axis_index("rad")
    nodes_z = plane_in.shape[1]
    nodes_x = dense.shape[0] // nodes_z
    elem_x, elem_z = potential.shape[:2]
    levels = rad * elem_z
    change = [cells[k // elem_z, k % elem_z] for k in range(levels)]
    shell = jnp.stack([6.0 + cells[k, elem_z] for k in range(rad)])
    forcing = jnp.stack(change + [jnp.zeros_like(change[0])] * rad)
    width, lanes = forcing.shape[1:]

    def apply_operator(values):
        gap = jnp.zeros_like(values[:1])
        neighbors = jnp.concatenate([values[1:], gap], axis=0)
        neighbors = neighbors + jnp.concatenate([gap, values[:-1]], axis=0)
        neighbors = neighbors + pltpu.roll(values, 1, 1) + pltpu.roll(values, width - 1, 1)
        neighbors = neighbors + pltpu.roll(values, 1, 2) + pltpu.roll(values, lanes - 1, 2)
        scaled = jnp.concatenate([6.0 * values[:levels], shell * values[levels:]], axis=0)
        return scaled - neighbors

    held[...] = smooth(forcing, apply_operator)[:levels]
    for f in range(elem_z):
        mine = held[r * elem_z + f]
        for e in range(elem_x):
            potential[e, f : f + 1, :] = mine[e : e + 1]

    row = lax.broadcasted_iota(jnp.int32, weight_zy.shape, 0)
    bottom = row == 0
    table = jnp.where(jnp.logical_and(bottom, r == 0), 0.5 * weight_zy[...], weight_zy[...])
    entering = jnp.logical_and(bottom, r > 0)
    base = [2.0 * WEIGHTS[0], WEIGHTS[1], WEIGHTS[2], WEIGHTS[3]]
    for x in range(nodes_x):
        here = slice(x * nodes_z, (x + 1) * nodes_z)
        gain = time_step / (dense[here] * (table * np.float32(base[x % 4])))
        for i in range(3):
            below = level_in[i, x : x + 1, :]
            if x == 0:
                below = below + level_in[i, nodes_x : nodes_x + 1, :]
            force = own_force[i, here] + jnp.where(entering, below, 0.0)
            if x == 0:
                force = force + plane_in[i]
            speed = velocity[i, here] + gain * (force + source[i, here])
            velocity_next[i, here] = speed
            disp_next[i, here] = disp[i, here] + time_step * speed


def on_device(surf, rad, displacement, velocity, source, lame_first, shear_modulus, density, shell_kappa):
    _, nodes_x, nodes_z, nodes_y = displacement.shape
    elem_x, elem_z, elem_y = nodes_x // 4, nodes_z // 4, nodes_y // 4
    own = nodes_x * nodes_z
    tile = elem_x * elem_z
    f32 = jnp.float32
    shape = jax.ShapeDtypeStruct
    pick = row_tables(nodes_x, nodes_z)
    fold = lane_tables(nodes_y)
    points, rows = pick.shape
    bf16 = functools.partial(jnp.asarray, dtype=jnp.bfloat16)
    plane, level = pl.pallas_call(
        functools.partial(halo_kernel, surf, rad),
        out_shape=[shape((6, nodes_z, nodes_y), f32), shape((6, nodes_x + 8, nodes_y), f32)],
        in_specs=[VMEM] * 4,
        out_specs=[VMEM] * 2,
        scratch_shapes=[
            pltpu.VMEM((6, nodes_z + nodes_x + 8, nodes_y), f32),
            pltpu.VMEM((6, nodes_z + nodes_x + 8, nodes_y), f32),
            pltpu.SemaphoreType.DMA((3,)),
            pltpu.SemaphoreType.DMA((3,)),
        ],
        compiler_params=pltpu.CompilerParams(
            collective_id=0, has_side_effects=True, vmem_limit_bytes=LIMIT
        ),
    )(displacement, lame_first, shear_modulus, density)

    flat = functools.partial(jnp.reshape, shape=(3, own, nodes_y))
    flat_material = functools.partial(jnp.reshape, shape=(own, nodes_y))
    weight = np.einsum("a,b,c->abc", WEIGHTS, WEIGHTS, WEIGHTS).reshape(-1).astype(np.float32)
    own_force, plane_out, level_out, payload = pl.pallas_call(
        functools.partial(element_kernel, elem_x, elem_z),
        out_shape=[
            shape((3, own, nodes_y), f32),
            shape((3, nodes_z, nodes_y), f32),
            shape((3, nodes_x + 8, nodes_y), f32),
            shape((elem_z + 1, elem_x, elem_y), f32),
        ],
        in_specs=[VMEM] * 11 + [SMEM],
        out_specs=[VMEM] * 4,
        scratch_shapes=[
            pltpu.VMEM((6, points, 5 * elem_y), f32),
            pltpu.VMEM((6, points, 5 * elem_y), f32),
            pltpu.VMEM((5, points, 5 * elem_y), f32),
            pltpu.VMEM((3, points, 5 * elem_y), f32),
        ],
        compiler_params=pltpu.CompilerParams(vmem_limit_bytes=LIMIT),
    )(
        flat(displacement),
        flat_material(lame_first),
        flat_material(shear_modulus),
        flat_material(density),
        shell_kappa,
        plane,
        level,
        bf16(fold[:nodes_y].T),
        bf16(fold),
        bf16(pick.T),
        bf16(np.concatenate([pick] * 3, axis=1)),
        jnp.asarray(weight),
    )

    peers = surf * rad
    plane_in, level_in, cells = pl.pallas_call(
        functools.partial(exchange_kernel, surf, rad),
        out_shape=[
            shape((3, nodes_z, nodes_y), f32),
            shape((3, nodes_x + 8, nodes_y), f32),
            shape((rad, elem_z + 1, surf, elem_x, elem_y), f32),
        ],
        in_specs=[VMEM] * 3,
        out_specs=[VMEM] * 3,
        scratch_shapes=[
            pltpu.SemaphoreType.DMA((3,)),
            pltpu.SemaphoreType.DMA((3,)),
            pltpu.SemaphoreType.DMA((peers,)),
            pltpu.SemaphoreType.DMA((peers,)),
        ],
        compiler_params=pltpu.CompilerParams(
            collective_id=1, has_side_effects=True, vmem_limit_bytes=LIMIT
        ),
    )(plane_out, level_out, payload)

    line = np.array([2.0 * WEIGHTS[0], WEIGHTS[1], WEIGHTS[2], WEIGHTS[3]])
    weight_zy = np.outer(np.tile(line, elem_z), np.tile(line, elem_y)).astype(np.float32)
    disp_next, velocity_next, potential = pl.pallas_call(
        functools.partial(finish_kernel, rad),
        out_shape=[
            shape((3, own, nodes_y), f32),
            shape((3, own, nodes_y), f32),
            shape((elem_x, elem_z, elem_y), f32),
        ],
        in_specs=[VMEM] * 9,
        out_specs=[VMEM] * 3,
        scratch_shapes=[pltpu.VMEM((rad * elem_z, surf * elem_x, elem_y), f32)],
        compiler_params=pltpu.CompilerParams(vmem_limit_bytes=LIMIT),
    )(
        flat(displacement),
        flat(velocity),
        flat(source),
        flat_material(density),
        own_force,
        plane_in,
        level_in,
        cells.reshape(rad, elem_z + 1, surf * elem_x, elem_y),
        jnp.asarray(weight_zy),
    )
    return (
        disp_next.reshape(displacement.shape),
        velocity_next.reshape(displacement.shape),
        potential,
    )


def solution(mesh):
    in_specs = (
        P(None, "surf", "rad", None),
        P(None, "surf", "rad", None),
        P(None, "surf", "rad", None),
        P("surf", "rad", None),
        P("surf", "rad", None),
        P("surf", "rad", None),
        P("surf", None, None),
    )
    out_specs = (P(None, "surf", "rad", None), P(None, "surf", "rad", None), P("surf", "rad", None))
    return jax.shard_map(
        functools.partial(on_device, mesh.shape["surf"], mesh.shape["rad"]),
        mesh=mesh,
        in_specs=in_specs,
        out_specs=out_specs,
        check_vma=False,
    )
```

profile of v0, /device:TPU:0, one launch (start us, length us, event | category | flops | bytes accessed | tf_op | source)
XLA Modules:
  0.0 42.8 jit_solution(10703718239497647229)
XLA Ops:
  0.6 0.0 copy-start
  0.6 1.1 %copy-done = f32[3,16,8,512]{3,2,1,0:T(8,128)S(1)} copy-done((f32[3,16,8,512]{3,2,1,0:T(8,128)S(1)}, f32[3,16,8,512]{3,2,1,0:T(8,128)}, u32[]{:S(2)}) %copy-start) | copy-done | bytes 786456
  1.8 0.0 copy-start.2
  1.8 0.9 %copy-done.2 = f32[16,8,512]{2,1,0:T(8,128)S(1)} copy-done((f32[16,8,512]{2,1,0:T(8,128)S(1)}, f32[16,8,512]{2,1,0:T(8,128)}, u32[]{:S(2)}) %copy-start.2) | copy-done | bytes 262168
  2.7 0.0 copy-start.4
  2.7 0.9 %copy-done.4 = f32[16,8,512]{2,1,0:T(8,128)S(1)} copy-done((f32[16,8,512]{2,1,0:T(8,128)S(1)}, f32[16,8,512]{2,1,0:T(8,128)}, u32[]{:S(2)}) %copy-start.4) | copy-done | bytes 262168
  3.7 0.0 copy-start.5
  3.7 0.9 %copy-done.5 = f32[16,8,512]{2,1,0:T(8,128)S(1)} copy-done((f32[16,8,512]{2,1,0:T(8,128)S(1)}, f32[16,8,512]{2,1,0:T(8,128)}, u32[]{:S(2)}) %copy-start.5) | copy-done | bytes 262168
  4.6 0.0 copy-start.8
  4.6 0.0 copy-start.9
  4.6 0.0 copy-start.10
  4.6 0.0 copy-start.11
  4.6 0.0 copy-start.13
  4.6 10.9 %shard_map.148 = (f32[6,8,512]{2,1,0:T(8,128)S(1)}, f32[6,24,512]{2,1,0:T(8,128)S(1)}) custom-call(f32[3,16,8,512]{3,2,1,0:T(8,128)S(1)} %copy-done, f32[16,8,512]{2,1,0:T(8,128)S(1)} %copy-done.4, f32[16,8,512]{2,1,0:T(8,128)S(1)} %copy-done.5, f32[16,8,512]{2,1,0:T(8,128)S(1)} %copy-done.2), custom_call_target="tpu_custom_call" | custom-call | tf_op jit(solution)/shard_map/pallas_call | solution.py:479
  15.5 0.0 copy-start.14
  15.5 0.0 copy-done.8
  15.5 0.0 copy-done.9
  15.5 0.0 copy-done.10
  15.5 0.0 copy-done.11
  15.6 0.0 copy-done.13
  15.6 0.6 %copy-done.14 = f32[125]{0:T(128)S(1)} copy-done((f32[125]{0:T(128)S(1)}, f32[125]{0:T(128)}, u32[]{:S(2)}) %copy-start.14) | copy-done | bytes 524
  16.2 0.0 copy-start.1
  16.2 0.0 copy-start.3
  16.2 0.0 copy-start.6
  16.2 0.0 copy-start.7
  16.2 10.6 %shard_map.149 = (f32[3,128,512]{2,1,0:T(8,128)S(1)}, f32[3,8,512]{2,1,0:T(8,128)S(1)}, f32[3,24,512]{2,1,0:T(8,128)S(1)}, f32[3,4,128]{2,1,0:T(4,128)S(1)}) custom-call(f32[3,128,512]{2,1,0:T(8,128)S(1)} %bitcast.9, f32[128,512]{1,0:T(8,128)S(1)} %bitcast.13, f32[128,512]{1,0:T(8,128)S(1)} %bitcast.14, f32[128,512]{1,0:T(8,128)S(1)} %bitcast.11, ...), custom_call_target="tpu_custom_call" | custom-call | tf_op jit(solution)/shard_map/pallas_call | solution.py:498
  26.8 0.0 copy-start.12
  26.8 13.5 %shard_map.150 = (f32[3,8,512]{2,1,0:T(8,128)S(1)}, f32[3,24,512]{2,1,0:T(8,128)S(1)}, f32[4,3,8,4,128]{4,3,2,1,0:T(4,128)S(1)}) custom-call(f32[3,8,512]{2,1,0:T(8,128)S(1)} %get-tuple-element.18.plane, f32[3,24,512]{2,1,0:T(8,128)S(1)} %get-tuple-element.19.level, f32[3,4,128]{2,1,0:T(4,128)S(1)} %get-tuple-element.20.payload), custom_call_target="tpu_custom_call" | custom-call | tf_op jit(solution)/shard_map/pallas_call | solution.py:531
  40.3 0.0 copy-done.1
  40.3 0.0 copy-done.3
  40.3 0.0 copy-done.6
  40.4 0.0 copy-done.7
  40.4 0.0 copy-done.12
  40.4 2.4 %shard_map.151 = (f32[3,128,512]{2,1,0:T(8,128)}, f32[3,128,512]{2,1,0:T(8,128)}, f32[4,2,128]{2,1,0:T(2,128)}) custom-call(f32[3,128,512]{2,1,0:T(8,128)S(1)} %bitcast.10, f32[3,128,512]{2,1,0:T(8,128)S(1)} %bitcast.15, f32[3,128,512]{2,1,0:T(8,128)S(1)} %bitcast.16, f32[128,512]{1,0:T(8,128)S(1)} %bitcast.12, ...), custom_call_target="tpu_custom_call" | custom-call | tf_op jit(solution)/shard_map/pallas_call | solution.py:553
Async XLA Ops:
  0.6 1.1 %copy-start = (f32[3,16,8,512]{3,2,1,0:T(8,128)S(1)}, f32[3,16,8,512]{3,2,1,0:T(8,128)}, u32[]{:S(2)}) copy-start(f32[3,16,8,512]{3,2,1,0:T(8,128)} %disp.1) | copy-start | bytes 2359300
  1.8 0.9 %copy-start.2 = (f32[16,8,512]{2,1,0:T(8,128)S(1)}, f32[16,8,512]{2,1,0:T(8,128)}, u32[]{:S(2)}) copy-start(f32[16,8,512]{2,1,0:T(8,128)} %dense.1) | copy-start | bytes 786436
  2.7 0.9 %copy-start.4 = (f32[16,8,512]{2,1,0:T(8,128)S(1)}, f32[16,8,512]{2,1,0:T(8,128)}, u32[]{:S(2)}) copy-start(f32[16,8,512]{2,1,0:T(8,128)} %lame.1) | copy-start | bytes 786436
  3.7 0.9 %copy-start.5 = (f32[16,8,512]{2,1,0:T(8,128)S(1)}, f32[16,8,512]{2,1,0:T(8,128)}, u32[]{:S(2)}) copy-start(f32[16,8,512]{2,1,0:T(8,128)} %shear.1) | copy-start | bytes 786436
  4.6 10.9 %copy-start.8 = (bf16[640,512]{1,0:T(8,128)(2,1)S(1)}, bf16[640,512]{1,0:T(8,128)(2,1)}, u32[]{:S(2)}) copy-start(bf16[640,512]{1,0:T(8,128)(2,1)} %constant.13.clone.fold) | copy-start | bytes 1966084
  4.6 10.9 %copy-start.9 = (bf16[512,512]{1,0:T(8,128)(2,1)S(1)}, bf16[512,512]{1,0:T(8,128)(2,1)}, u32[]{:S(2)}) copy-start(bf16[512,512]{1,0:T(8,128)(2,1)} %constant.12.clone.unfold) | copy-start | bytes 1572868
  4.6 10.9 %copy-start.10 = (bf16[208,480]{1,0:T(8,128)(2,1)S(1)}, bf16[208,480]{1,0:T(8,128)(2,1)}, u32[]{:S(2)}) copy-start(bf16[208,480]{1,0:T(8,128)(2,1)} %constant.15.clone.gather) | copy-start | bytes 599044
  4.6 10.9 %copy-start.11 = (bf16[160,208]{1,0:T(8,128)(2,1)S(1)}, bf16[160,208]{1,0:T(8,128)(2,1)}, u32[]{:S(2)}) copy-start(bf16[160,208]{1,0:T(8,128)(2,1)} %constant.14.clone.pick) | copy-start | bytes 199684
  4.6 10.9 %copy-start.13 = (f32[4,4,128]{2,1,0:T(4,128)S(1)}, f32[4,4,128]{2,1,0:T(4,128)}, u32[]{:S(2)}) copy-start(f32[4,4,128]{2,1,0:T(4,128)} %kappa.1) | copy-start | bytes 24580
  15.5 0.7 %copy-start.14 = (f32[125]{0:T(128)S(1)}, f32[125]{0:T(128)}, u32[]{:S(2)}) copy-start(f32[125]{0:T(128)} %constant.16.clone.weight) | copy-start | bytes 1504
  16.2 24.2 %copy-start.1 = (f32[3,16,8,512]{3,2,1,0:T(8,128)S(1)}, f32[3,16,8,512]{3,2,1,0:T(8,128)}, u32[]{:S(2)}) copy-start(f32[3,16,8,512]{3,2,1,0:T(8,128)} %disp.1) | copy-start | bytes 2359300
  16.2 24.2 %copy-start.3 = (f32[16,8,512]{2,1,0:T(8,128)S(1)}, f32[16,8,512]{2,1,0:T(8,128)}, u32[]{:S(2)}) copy-start(f32[16,8,512]{2,1,0:T(8,128)} %dense.1) | copy-start | bytes 786436
  16.2 24.2 %copy-start.6 = (f32[3,16,8,512]{3,2,1,0:T(8,128)S(1)}, f32[3,16,8,512]{3,2,1,0:T(8,128)}, u32[]{:S(2)}) copy-start(f32[3,16,8,512]{3,2,1,0:T(8,128)} %param.14) | copy-start | bytes 2359300
  16.2 24.2 %copy-start.7 = (f32[3,16,8,512]{3,2,1,0:T(8,128)S(1)}, f32[3,16,8,512]{3,2,1,0:T(8,128)}, u32[]{:S(2)}) copy-start(f32[3,16,8,512]{3,2,1,0:T(8,128)} %param.15) | copy-start | bytes 2359300
  26.8 13.5 %copy-start.12 = (f32[8,512]{1,0:T(8,128)S(1)}, f32[8,512]{1,0:T(8,128)}, u32[]{:S(2)}) copy-start(f32[8,512]{1,0:T(8,128)} %constant.17.clone.weight_zy) | copy-start | bytes 49156
where the time goes:
time: 43 us; the launch traced here: 42.8 us
  Pallas kernels  37.4 us (87%)
  local copies, waits for them, and re-layouts  4.62 us (11%)
  between operations  0.78 us (2%)
    pallas_call x1, Pallas kernels, on_device(): pl.pallas_call(functools.partial(exchange_kernel, surf, rad), out_shape=[...  13.5 us
    pallas_call x1, Pallas kernels, on_device(): pl.pallas_call(functools.partial(halo_kernel, surf, rad), out_shape=[shap...  10.9 us
    pallas_call x1, Pallas kernels, on_device(): pl.pallas_call(functools.partial(element_kernel, elem_x, elem_z), out_sha...  10.6 us
    unnamed x30, local copies, waits for them, and re-layouts  4.62 us
    pallas_call x1, Pallas kernels, on_device(): pl.pallas_call(functools.partial(finish_kernel, rad), out_shape=[shape((3...  2.4 us

commit v1 on v0

v1 whole, which is shorter than its diff:
```python
import functools

import jax
import jax.numpy as jnp
import numpy as np
from jax import lax
from jax.experimental import pallas as pl
from jax.experimental.pallas import tpu as pltpu
from jax.sharding import PartitionSpec as P

CYCLES = 2
STEPS = 3

time_step = 0.005
coupling = 4.0
upper_margin = 1.1
spectrum_ratio = 10.0
MESH = pl.DeviceIdType.MESH
VMEM = pl.BlockSpec(memory_space=pltpu.VMEM)
HBM = pl.BlockSpec(memory_space=pltpu.HBM)
LIMIT = 48 * 1024 * 1024


def node_tables():
    points = np.array([-1.0, -np.sqrt(3.0 / 7.0), 0.0, np.sqrt(3.0 / 7.0), 1.0])
    weights = np.array([0.1, 49.0 / 90.0, 32.0 / 45.0, 49.0 / 90.0, 0.1])
    scales = np.array(
        [
            np.prod([points[outer] - points[inner] for inner in range(5) if inner != outer])
            for outer in range(5)
        ]
    )
    derivative = np.zeros((5, 5))
    for row_index in range(5):
        for col_index in range(5):
            if row_index != col_index:
                derivative[row_index, col_index] = (
                    scales[row_index] / scales[col_index] / (points[row_index] - points[col_index])
                )
            else:
                derivative[row_index, col_index] = sum(
                    (
                        1.0 / (points[col_index] - points[inner])
                        for inner in range(5)
                        if inner != col_index
                    )
                )
    return (derivative, weights)


DERIVATIVE, WEIGHTS = node_tables()


def line_product(matrix, u):
    u0, u1, u2, u3, u4 = u
    s0, d0, s1, d1 = u0 + u4, u0 - u4, u1 + u3, u1 - u3

    def scaled(terms):
        total = None
        for factor, value in terms:
            if abs(factor) < 1e-12:
                continue
            term = value * np.float32(factor)
            total = term if total is None else total + term
        return total

    even = [
        scaled(
            [
                (0.5 * (matrix[p, 0] + matrix[p, 4]), s0),
                (0.5 * (matrix[p, 1] + matrix[p, 3]), s1),
                (matrix[p, 2], u2),
            ]
        )
        for p in range(2)
    ]
    odd = [
        scaled(
            [
                (0.5 * (matrix[p, 0] - matrix[p, 4]), d0),
                (0.5 * (matrix[p, 1] - matrix[p, 3]), d1),
            ]
        )
        for p in range(3)
    ]
    return [even[0] + odd[0], even[1] + odd[1], odd[2], odd[1] - even[1], odd[0] - even[0]]


def three_parts(values):
    high = values.astype(jnp.bfloat16)
    rest = values - high.astype(jnp.float32)
    middle = rest.astype(jnp.bfloat16)
    low = (rest - middle.astype(jnp.float32)).astype(jnp.bfloat16)
    return high, middle, low


def two_parts(values):
    high = values.astype(jnp.bfloat16)
    return high, (values - high.astype(jnp.float32)).astype(jnp.bfloat16)


def dot(first, second):
    return jnp.dot(first, second, preferred_element_type=jnp.float32)


def row_tables(nodes_x, nodes_z):
    own = nodes_x * nodes_z
    elem_x, elem_z = nodes_x // 4, nodes_z // 4
    tile = elem_x * elem_z
    rows = own + nodes_z + nodes_x + 8
    points = -(-25 * tile // 16) * 16
    pick = np.zeros((points, rows), np.float32)
    for a in range(5):
        for b in range(5):
            for f in range(elem_z):
                for e in range(elem_x):
                    x, z = 4 * e + a, 4 * f + b
                    if x < nodes_x and z < nodes_z:
                        row = x * nodes_z + z
                    elif z < nodes_z:
                        row = own + z
                    elif x < nodes_x:
                        row = own + nodes_z + x
                    else:
                        row = own + nodes_z + nodes_x
                    pick[(a * 5 + b) * tile + f * elem_x + e, row] = 1.0
    return pick


def lane_tables(nodes_y):
    elem_y = nodes_y // 4
    fold = np.zeros((5 * elem_y, nodes_y), np.float32)
    for c in range(5):
        for g in range(elem_y):
            fold[c * elem_y + g, (4 * g + c) % nodes_y] = 1.0
    return fold


def step_kernel(
    surf,
    rad,
    nodes_x,
    nodes_z,
    disp,
    lame,
    shear,
    dense,
    kappa_in,
    unfold_in,
    fold_in,
    pick_in,
    gather_in,
    own_out,
    plane_in,
    level_in,
    potential,
    fields,
    level_send,
    kappa,
    unfold,
    fold,
    pick,
    gather,
    lanes,
    views,
    grads,
    terms,
    force,
    merged,
    edge,
    cells,
    lattice,
    load_sem,
    halo_send,
    halo_recv,
    column_send,
    column_recv,
    line_send,
    line_recv,
    force_send,
    force_recv,
):
    s, r = lax.axis_index("surf"), lax.axis_index("rad")
    own, nodes_y = lame.shape
    elem_x, elem_z, elem_y = nodes_x // 4, nodes_z // 4, nodes_y // 4
    tile = elem_x * elem_z
    rows_all, points = pick.shape
    edge_rows = rows_all - own

    def line_peer(k):
        return lax.rem(s + k, surf), r

    def column_peer(k):
        return s, lax.rem(r + k, rad)

    low = lax.rem(s + surf - 1, surf), lax.rem(r + rad - 1, rad)
    high = lax.rem(s + 1, surf), lax.rem(r + 1, rad)
    barrier = pltpu.get_barrier_semaphore()

    def greet(target):
        pl.semaphore_signal(barrier, inc=1, device_id=target, device_id_type=MESH)

    def greet_line(k, carry):
        greet(line_peer(k))
        return carry

    loads = [(disp.at[i], fields.at[i, pl.ds(0, own)]) for i in range(3)]
    loads += [(ref, fields.at[3 + i, pl.ds(0, own)]) for i, ref in enumerate((lame, shear, dense))]
    loads += [(unfold_in, unfold), (gather_in, gather), (pick_in, pick), (fold_in, fold)]
    loads += [(kappa_in, kappa)]
    loads = [
        pltpu.make_async_copy(source, target, load_sem.at[k])
        for k, (source, target) in enumerate(loads)
    ]
    for load in loads:
        load.start()
    greet(low)
    greet(high)
    for k in range(1, rad):
        greet(column_peer(k))
    lax.fori_loop(1, surf, greet_line, 0)

    for load in loads[:6]:
        load.wait()
    for i in range(6):
        for x in range(nodes_x):
            level_send[i, x : x + 1, :] = fields[i, x * nodes_z : x * nodes_z + 1, :]
    pl.semaphore_wait(barrier, surf + rad)

    def remote(source, target, sems, k, peer):
        return pltpu.make_async_remote_copy(
            src_ref=source,
            dst_ref=target,
            send_sem=sems[0].at[k],
            recv_sem=sems[1].at[k],
            device_id=peer,
            device_id_type=MESH,
        )

    halo = (halo_send, halo_recv)
    first = fields.at[:, pl.ds(0, nodes_z)]
    halos = [
        remote(first, fields.at[:, pl.ds(own, nodes_z)], halo, 0, (low[0], r)),
        remote(level_send, fields.at[:, pl.ds(own + nodes_z, nodes_x)], halo, 1, (s, low[1])),
        remote(
            fields.at[:, pl.ds(0, 8)], fields.at[:, pl.ds(own + nodes_z + nodes_x, 8)], halo, 2, low
        ),
    ]
    for copy in halos:
        copy.start()
    for load in loads[6:]:
        load.wait()
    for i in range(6):
        split = jnp.concatenate(three_parts(fields[i, :own]), axis=0)
        spread = dot(split, unfold[...]).astype(jnp.bfloat16)
        for part in range(3):
            lanes[i, part * rows_all : part * rows_all + own] = spread[part * own : (part + 1) * own]
    for copy in halos:
        copy.wait_recv()
    split = []
    for i in range(6):
        outer = jnp.where(r == rad - 1, 0.0, fields[i, own + nodes_z :])
        split += three_parts(jnp.concatenate([fields[i, own : own + nodes_z], outer], axis=0))
    spread = dot(jnp.concatenate(split, axis=0), unfold[...]).astype(jnp.bfloat16)
    for i in range(6):
        for part in range(3):
            start = (3 * i + part) * edge_rows
            lanes[i, part * rows_all + own : (part + 1) * rows_all] = spread[
                start : start + edge_rows
            ]
    for i in range(6):
        picked = dot(gather[...], lanes[i])
        views[i, :, :nodes_y] = picked
        views[i, :, nodes_y:] = pltpu.roll(picked[:, :elem_y], elem_y - 1, 1)

    def rows(a, b):
        return pl.ds(pl.multiple_of((a * 5 + b) * tile, tile), tile)

    def lanes_of(c):
        return pl.ds(c * elem_y, elem_y)

    def x_gradients(b, carry):
        for c in range(5):
            for i in range(3):
                line = [views[i, rows(a, b), lanes_of(c)] for a in range(5)]
                for a, value in enumerate(line_product(DERIVATIVE, line)):
                    grads[i, rows(a, b), lanes_of(c)] = value
        return carry

    lax.fori_loop(0, 5, x_gradients, 0)

    def stresses(a, total):
        outer_weight = jnp.where(
            jnp.logical_or(a == 0, a == 4),
            np.float32(WEIGHTS[0]),
            jnp.where(a == 2, np.float32(WEIGHTS[2]), np.float32(WEIGHTS[1])),
        )
        outer_weight = jnp.full((tile, elem_y), outer_weight, jnp.float32)
        for c in range(5):
            for i in range(3):
                line = [views[i, rows(a, b), lanes_of(c)] for b in range(5)]
                for b, value in enumerate(line_product(DERIVATIVE, line)):
                    grads[3 + i, rows(a, b), lanes_of(c)] = value
        for b in range(5):
            here = rows(a, b)
            along = [
                line_product(DERIVATIVE, [views[i, here, lanes_of(c)] for c in range(5)])
                for i in range(3)
            ]
            toward = [[], [], []]
            for c in range(5):
                scale = outer_weight * np.float32(WEIGHTS[b] * WEIGHTS[c])
                mu = views[4, here, lanes_of(c)] * scale
                x0, x1, x2 = [grads[i, here, lanes_of(c)] for i in range(3)]
                z0, z1, z2 = [grads[3 + i, here, lanes_of(c)] for i in range(3)]
                y0, y1, y2 = [along[i][c] for i in range(3)]
                dilatation = (x0 + z1) + y2
                total = total + (views[5, here, lanes_of(c)] * scale) * dilatation
                bulk = (views[3, here, lanes_of(c)] * scale) * dilatation
                double = mu + mu
                terms[0, here, lanes_of(c)] = double * x0 + bulk
                terms[1, here, lanes_of(c)] = mu * (x1 + z0)
                terms[2, here, lanes_of(c)] = mu * (x2 + y0)
                terms[3, here, lanes_of(c)] = double * z1 + bulk
                terms[4, here, lanes_of(c)] = mu * (z2 + y1)
                toward[0].append(mu * (x2 + y0))
                toward[1].append(mu * (z2 + y1))
                toward[2].append(double * y2 + bulk)
            for i in range(3):
                for c, value in enumerate(line_product(-DERIVATIVE.T, toward[i])):
                    force[i, here, lanes_of(c)] = value
        return total

    total = lax.fori_loop(0, 5, stresses, jnp.zeros((tile, elem_y), jnp.float32))
    change = -coupling * total
    for f in range(elem_z):
        cells[r, f, 0] = change[f * elem_x : (f + 1) * elem_x]
    shell = jnp.zeros((elem_x, elem_y), jnp.float32)
    for k in range(kappa.shape[1]):
        level_rows = jnp.concatenate([kappa[e, k : k + 1, :] for e in range(elem_x)], axis=0)
        shell = jnp.where(r == k, level_rows, shell)
    cells[r, elem_z, 0] = shell

    column = (column_send, column_recv)
    line = (line_send, line_recv)

    def column_copy(k, owner):
        return remote(cells.at[r, :, 0], cells.at[owner, :, 0], column, k, column_peer(k))

    def line_copy(k):
        return remote(cells.at[:, :, 0], cells.at[:, :, surf - k], line, k, line_peer(k))

    for k in range(1, rad):
        column_copy(k, r).start()

    def z_forces(a, carry):
        for c in range(5):
            for i, term in enumerate((1, 3, 4)):
                values = [terms[term, rows(a, b), lanes_of(c)] for b in range(5)]
                for b, value in enumerate(line_product(-DERIVATIVE.T, values)):
                    force[i, rows(a, b), lanes_of(c)] += value
        return carry

    lax.fori_loop(0, 5, z_forces, 0)

    def x_forces(b, carry):
        for c in range(5):
            for i in range(3):
                values = [terms[i, rows(a, b), lanes_of(c)] for a in range(5)]
                for a, value in enumerate(line_product(-DERIVATIVE.T, values)):
                    force[i, rows(a, b), lanes_of(c)] += value
        return carry

    lax.fori_loop(0, 5, x_forces, 0)
    for k in range(1, rad):
        column_copy(k, lax.rem(r + rad - k, rad)).wait_recv()

    def begin_line(k, carry):
        line_copy(k).start()
        return carry

    lax.fori_loop(1, surf, begin_line, 0)
    if points > 25 * tile:
        force[:, 25 * tile :, :] = jnp.zeros((3, points - 25 * tile, 5 * elem_y), jnp.float32)
    for i in range(3):
        total = sum(dot(pick[...], part) for part in two_parts(force[i]))
        high_part, low_part = two_parts(total)
        merged[0, i] = high_part
        merged[1, i] = low_part
    split = [merged[part, i, own:] for part in range(2) for i in range(3)]
    whole = dot(jnp.concatenate(split, axis=0), fold[...])
    for i in range(3):
        edge[i] = (
            whole[i * edge_rows : (i + 1) * edge_rows]
            + whole[(3 + i) * edge_rows : (4 + i) * edge_rows]
        )
    sems = (force_send, force_recv)
    upper = pl.ds(nodes_z, nodes_x)
    last = pl.ds(nodes_z + nodes_x, 8)
    pushes = [
        remote(edge.at[:, pl.ds(0, nodes_z)], plane_in, sems, 0, (high[0], r)),
        remote(edge.at[:, upper], level_in.at[:, pl.ds(0, nodes_x)], sems, 1, (s, high[1])),
        remote(edge.at[:, last], level_in.at[:, pl.ds(nodes_x, 8)], sems, 2, high),
    ]
    for copy in pushes:
        copy.start()
    for i in range(3):
        whole = dot(jnp.concatenate([merged[part, i, :own] for part in range(2)], axis=0), fold[...])
        own_out[i] = whole[:own] + whole[own:]

    def finish_line(k, carry):
        copy = line_copy(k)
        copy.wait_recv()
        copy.wait_send()
        return carry

    lax.fori_loop(1, surf, finish_line, 0)
    levels = rad * elem_z
    for k in range(rad):
        for f in range(elem_z + 1):
            level = k * elem_z + f if f < elem_z else levels + k
            for block in range(surf):
                lattice[level, block * elem_x : (block + 1) * elem_x] = cells[k, f, block]
    shell = 6.0 + lattice[levels:]
    forcing = jnp.concatenate([lattice[:levels], jnp.zeros_like(shell)], axis=0)
    width, depth = forcing.shape[1:]

    def apply_operator(values):
        gap = jnp.zeros_like(values[:1])
        neighbors = jnp.concatenate([values[1:], gap], axis=0)
        neighbors = neighbors + jnp.concatenate([gap, values[:-1]], axis=0)
        neighbors = neighbors + pltpu.roll(values, 1, 1) + pltpu.roll(values, width - 1, 1)
        neighbors = neighbors + pltpu.roll(values, 1, 2) + pltpu.roll(values, depth - 1, 2)
        scaled = jnp.concatenate([6.0 * values[:levels], shell * values[levels:]], axis=0)
        return scaled - neighbors

    lattice[:levels] = smooth(forcing, apply_operator)[:levels]
    for f in range(elem_z):
        potential[f] = lattice[r * elem_z + f, :elem_x]
    for copy in halos:
        copy.wait_send()
    for k in range(1, rad):
        column_copy(k, r).wait_send()
    for copy in pushes:
        copy.wait()


def smooth(forcing, apply_operator):
    def total(values):
        return jnp.sum(jnp.sum(values, axis=0), axis=(0, 1), keepdims=True)[None]

    potential_all = jnp.zeros_like(forcing)
    residual = forcing
    for cycle_index in range(CYCLES):
        applied = apply_operator(residual)
        upper_bound = upper_margin * total(applied * applied) / total(residual * applied)
        lower_bound = upper_bound / spectrum_ratio
        midpoint = 0.5 * (upper_bound + lower_bound)
        half_width = 0.5 * (upper_bound - lower_bound)
        spread = midpoint / half_width
        previous = 1.0 / spread
        inverse = 1.0 / midpoint
        correction = residual * inverse
        potential_all = potential_all + correction
        residual = residual - applied * inverse
        for step_index in range(1, STEPS):
            weighting = 1.0 / (2.0 * spread - previous)
            correction = (weighting * previous) * correction + (
                2.0 * weighting / half_width
            ) * residual
            previous = weighting
            potential_all = potential_all + correction
            if cycle_index < CYCLES - 1 or step_index < STEPS - 1:
                residual = residual - apply_operator(correction)
    return potential_all


def finish_kernel(
    disp,
    velocity,
    source,
    dense,
    own_force,
    plane_in,
    level_in,
    solved,
    weight_zy,
    disp_next,
    velocity_next,
    potential,
):
    r = lax.axis_index("rad")
    nodes_z = plane_in.shape[1]
    nodes_x = dense.shape[0] // nodes_z
    elem_x, elem_z = potential.shape[:2]
    for f in range(elem_z):
        for e in range(elem_x):
            potential[e, f : f + 1, :] = solved[f, e : e + 1, :]

    row = lax.broadcasted_iota(jnp.int32, weight_zy.shape, 0)
    bottom = row == 0
    table = jnp.where(jnp.logical_and(bottom, r == 0), 0.5 * weight_zy[...], weight_zy[...])
    entering = jnp.logical_and(bottom, r > 0)
    base = [2.0 * WEIGHTS[0], WEIGHTS[1], WEIGHTS[2], WEIGHTS[3]]
    for x in range(nodes_x):
        here = slice(x * nodes_z, (x + 1) * nodes_z)
        gain = time_step / (dense[here] * (table * np.float32(base[x % 4])))
        for i in range(3):
            below = level_in[i, x : x + 1, :]
            if x == 0:
                below = below + level_in[i, nodes_x : nodes_x + 1, :]
            force = own_force[i, here] + jnp.where(entering, below, 0.0)
            if x == 0:
                force = force + plane_in[i]
            speed = velocity[i, here] + gain * (force + source[i, here])
            velocity_next[i, here] = speed
            disp_next[i, here] = disp[i, here] + time_step * speed


def on_device(surf, rad, displacement, velocity, source, lame_first, shear_modulus, density, shell_kappa):
    _, nodes_x, nodes_z, nodes_y = displacement.shape
    elem_x, elem_z, elem_y = nodes_x // 4, nodes_z // 4, nodes_y // 4
    own = nodes_x * nodes_z
    f32 = jnp.float32
    shape = jax.ShapeDtypeStruct
    pick = row_tables(nodes_x, nodes_z)
    fold = lane_tables(nodes_y)
    points, rows = pick.shape
    bf16 = functools.partial(jnp.asarray, dtype=jnp.bfloat16)
    flat = functools.partial(jnp.reshape, shape=(3, own, nodes_y))
    flat_material = functools.partial(jnp.reshape, shape=(own, nodes_y))
    vmem = pltpu.VMEM
    dma = pltpu.SemaphoreType.DMA
    own_force, plane_in, level_in, solved = pl.pallas_call(
        functools.partial(step_kernel, surf, rad, nodes_x, nodes_z),
        out_shape=[
            shape((3, own, nodes_y), f32),
            shape((3, nodes_z, nodes_y), f32),
            shape((3, nodes_x + 8, nodes_y), f32),
            shape((elem_z, elem_x, elem_y), f32),
        ],
        in_specs=[HBM] * 9,
        out_specs=[VMEM] * 4,
        scratch_shapes=[
            vmem((6, rows, nodes_y), f32),
            vmem((6, nodes_x, nodes_y), f32),
            vmem(shell_kappa.shape, f32),
            vmem((nodes_y, nodes_y), jnp.bfloat16),
            vmem((5 * elem_y, nodes_y), jnp.bfloat16),
            vmem((rows, points), jnp.bfloat16),
            vmem((points, 3 * rows), jnp.bfloat16),
            vmem((6, 3 * rows, nodes_y), jnp.bfloat16),
            vmem((6, points, 5 * elem_y), f32),
            vmem((6, points, 5 * elem_y), f32),
            vmem((5, points, 5 * elem_y), f32),
            vmem((3, points, 5 * elem_y), f32),
            vmem((2, 3, rows, 5 * elem_y), jnp.bfloat16),
            vmem((3, rows - own, nodes_y), f32),
            vmem((rad, elem_z + 1, surf, elem_x, elem_y), f32),
            vmem((rad * (elem_z + 1), surf * elem_x, elem_y), f32),
            dma((11,)),
            dma((3,)),
            dma((3,)),
            dma((rad,)),
            dma((rad,)),
            dma((surf,)),
            dma((surf,)),
            dma((3,)),
            dma((3,)),
        ],
        compiler_params=pltpu.CompilerParams(
            collective_id=0, has_side_effects=True, vmem_limit_bytes=LIMIT
        ),
    )(
        flat(displacement),
        flat_material(lame_first),
        flat_material(shear_modulus),
        flat_material(density),
        shell_kappa,
        bf16(fold[:nodes_y].T),
        bf16(fold),
        bf16(pick.T),
        bf16(np.concatenate([pick] * 3, axis=1)),
    )

    line = np.array([2.0 * WEIGHTS[0], WEIGHTS[1], WEIGHTS[2], WEIGHTS[3]])
    weight_zy = np.outer(np.tile(line, elem_z), np.tile(line, elem_y)).astype(np.float32)
    disp_next, velocity_next, potential = pl.pallas_call(
        finish_kernel,
        out_shape=[
            shape((3, own, nodes_y), f32),
            shape((3, own, nodes_y), f32),
            shape((elem_x, elem_z, elem_y), f32),
        ],
        in_specs=[VMEM] * 9,
        out_specs=[VMEM] * 3,
        compiler_params=pltpu.CompilerParams(vmem_limit_bytes=LIMIT),
    )(
        flat(displacement),
        flat(velocity),
        flat(source),
        flat_material(density),
        own_force,
        plane_in,
        level_in,
        solved,
        jnp.asarray(weight_zy),
    )
    return (
        disp_next.reshape(displacement.shape),
        velocity_next.reshape(displacement.shape),
        potential,
    )


def solution(mesh):
    in_specs = (
        P(None, "surf", "rad", None),
        P(None, "surf", "rad", None),
        P(None, "surf", "rad", None),
        P("surf", "rad", None),
        P("surf", "rad", None),
        P("surf", "rad", None),
        P("surf", None, None),
    )
    out_specs = (P(None, "surf", "rad", None), P(None, "surf", "rad", None), P("surf", "rad", None))
    return jax.shard_map(
        functools.partial(on_device, mesh.shape["surf"], mesh.shape["rad"]),
        mesh=mesh,
        in_specs=in_specs,
        out_specs=out_specs,
        check_vma=False,
    )
```

time: 43 us -> 40.3 us (0.937)
  Pallas kernels: 37.4 us -> 30.5 us
  local copies, waits for them, and re-layouts: 4.62 us -> 8.63 us
    pallas_call x4 -> x2, Pallas kernels: 37.4 us -> 30.5 us  [the longest x1 29 us: on_device(): pl.pallas_call(functools.partial(step_kernel, surf, rad, nodes_x, nodes_z...]
    unnamed x30 -> x26, local copies, waits for them, and re-layouts: 4.62 us -> 8.63 us
where the time goes in v1:
time: 40.3 us; the launch traced here: 39.8 us
  Pallas kernels  30.5 us (76%)
  local copies, waits for them, and re-layouts  8.63 us (21%)
  between operations  0.69 us (2%)
    pallas_call x1, Pallas kernels, on_device(): pl.pallas_call(functools.partial(step_kernel, surf, rad, nodes_x, nodes_z...  29 us
    unnamed x26, local copies, waits for them, and re-layouts  8.63 us
    pallas_call x1, Pallas kernels, on_device(): pl.pallas_call(finish_kernel, out_shape=[shape((3, own, nodes_y), f32), s...  1.47 us

profile of v1, /device:TPU:0, one launch (start us, length us, event | category | flops | bytes accessed | tf_op | source)
XLA Modules:
  0.0 39.8 jit_solution(11709812228200096570)
XLA Ops:
  0.6 0.0 copy-start.12
  0.6 0.7 %copy-done.12 = f32[4,4,128]{2,1,0:T(4,128)S(1)} copy-done((f32[4,4,128]{2,1,0:T(4,128)S(1)}, f32[4,4,128]{2,1,0:T(4,128)}, u32[]{:S(2)}) %copy-start.12) | copy-done | bytes 8216
  1.3 0.0 copy-start
  1.3 1.1 %copy-done = f32[3,16,8,512]{3,2,1,0:T(8,128)S(1)} copy-done((f32[3,16,8,512]{3,2,1,0:T(8,128)S(1)}, f32[3,16,8,512]{3,2,1,0:T(8,128)}, u32[]{:S(2)}) %copy-start) | copy-done | bytes 786456
  2.5 0.0 copy-start.1
  2.5 0.9 %copy-done.1 = f32[16,8,512]{2,1,0:T(8,128)S(1)} copy-done((f32[16,8,512]{2,1,0:T(8,128)S(1)}, f32[16,8,512]{2,1,0:T(8,128)}, u32[]{:S(2)}) %copy-start.1) | copy-done | bytes 262168
  3.4 0.0 copy-start.5
  3.4 1.1 %copy-done.5 = bf16[640,512]{1,0:T(8,128)(2,1)S(1)} copy-done((bf16[640,512]{1,0:T(8,128)(2,1)S(1)}, bf16[640,512]{1,0:T(8,128)(2,1)}, u32[]{:S(2)}) %copy-start.5) | copy-done | bytes 655384
  4.5 0.0 copy-start.6
  4.5 1.0 %copy-done.6 = bf16[512,512]{1,0:T(8,128)(2,1)S(1)} copy-done((bf16[512,512]{1,0:T(8,128)(2,1)S(1)}, bf16[512,512]{1,0:T(8,128)(2,1)}, u32[]{:S(2)}) %copy-start.6) | copy-done | bytes 524312
  5.5 0.0 copy-start.7
  5.5 0.9 %copy-done.7 = f32[16,8,512]{2,1,0:T(8,128)S(1)} copy-done((f32[16,8,512]{2,1,0:T(8,128)S(1)}, f32[16,8,512]{2,1,0:T(8,128)}, u32[]{:S(2)}) %copy-start.7) | copy-done | bytes 262168
  6.5 0.0 copy-start.8
  6.5 0.9 %copy-done.8 = f32[16,8,512]{2,1,0:T(8,128)S(1)} copy-done((f32[16,8,512]{2,1,0:T(8,128)S(1)}, f32[16,8,512]{2,1,0:T(8,128)}, u32[]{:S(2)}) %copy-start.8) | copy-done | bytes 262168
  7.4 0.0 copy-start.9
  7.4 0.9 %copy-done.9 = bf16[208,480]{1,0:T(8,128)(2,1)S(1)} copy-done((bf16[208,480]{1,0:T(8,128)(2,1)S(1)}, bf16[208,480]{1,0:T(8,128)(2,1)}, u32[]{:S(2)}) %copy-start.9) | copy-done | bytes 199704
  8.4 0.0 copy-start.10
  8.4 0.9 %copy-done.10 = bf16[160,208]{1,0:T(8,128)(2,1)S(1)} copy-done((bf16[160,208]{1,0:T(8,128)(2,1)S(1)}, bf16[160,208]{1,0:T(8,128)(2,1)}, u32[]{:S(2)}) %copy-start.10) | copy-done | bytes 66584
  9.3 0.0 copy-start.2
  9.3 0.0 copy-start.3
  9.3 0.0 copy-start.4
  9.3 0.0 copy-start.11
  9.3 29.0 %shard_map.139 = (f32[3,128,512]{2,1,0:T(8,128)S(1)}, f32[3,8,512]{2,1,0:T(8,128)S(1)}, f32[3,24,512]{2,1,0:T(8,128)S(1)}, f32[2,4,128]{2,1,0:T(4,128)S(1)}) custom-call(f32[3,128,512]{2,1,0:T(8,128)S(1)} %bitcast.8, f32[128,512]{1,0:T(8,128)S(1)} %bitcast.14, f32[128,512]{1,0:T(8,128)S(1)} %bitcast.15, f32[128,512]{1,0:T(8,128)S(1)} %bitcast.10, ...), custom_call_target="tpu_custom_call" | custom-call | tf_op jit(solution)/shard_map/pallas_call | solution.py:534
  38.3 0.0 copy-done.2
  38.3 0.0 copy-done.3
  38.3 0.0 copy-done.4
  38.3 0.0 copy-done.11
  38.3 1.5 %shard_map.140 = (f32[3,128,512]{2,1,0:T(8,128)}, f32[3,128,512]{2,1,0:T(8,128)}, f32[4,2,128]{2,1,0:T(2,128)}) custom-call(f32[3,128,512]{2,1,0:T(8,128)S(1)} %bitcast.9, f32[3,128,512]{2,1,0:T(8,128)S(1)} %bitcast.12, f32[3,128,512]{2,1,0:T(8,128)S(1)} %bitcast.13, f32[128,512]{1,0:T(8,128)S(1)} %bitcast.11, ...), custom_call_target="tpu_custom_call" | custom-call | tf_op jit(solution)/shard_map/pallas_call | solution.py:588
Async XLA Ops:
  0.6 0.7 %copy-start.12 = (f32[4,4,128]{2,1,0:T(4,128)S(1)}, f32[4,4,128]{2,1,0:T(4,128)}, u32[]{:S(2)}) copy-start(f32[4,4,128]{2,1,0:T(4,128)} %kappa_in.1) | copy-start | bytes 24580
  1.3 1.1 %copy-start = (f32[3,16,8,512]{3,2,1,0:T(8,128)S(1)}, f32[3,16,8,512]{3,2,1,0:T(8,128)}, u32[]{:S(2)}) copy-start(f32[3,16,8,512]{3,2,1,0:T(8,128)} %param.12) | copy-start | bytes 2359300
  2.5 0.9 %copy-start.1 = (f32[16,8,512]{2,1,0:T(8,128)S(1)}, f32[16,8,512]{2,1,0:T(8,128)}, u32[]{:S(2)}) copy-start(f32[16,8,512]{2,1,0:T(8,128)} %param.17) | copy-start | bytes 786436
  3.4 1.1 %copy-start.5 = (bf16[640,512]{1,0:T(8,128)(2,1)S(1)}, bf16[640,512]{1,0:T(8,128)(2,1)}, u32[]{:S(2)}) copy-start(bf16[640,512]{1,0:T(8,128)(2,1)} %constant.11.clone.fold_in) | copy-start | bytes 1966084
  4.5 1.0 %copy-start.6 = (bf16[512,512]{1,0:T(8,128)(2,1)S(1)}, bf16[512,512]{1,0:T(8,128)(2,1)}, u32[]{:S(2)}) copy-start(bf16[512,512]{1,0:T(8,128)(2,1)} %constant.10.clone.unfold_in) | copy-start | bytes 1572868
  5.5 0.9 %copy-start.7 = (f32[16,8,512]{2,1,0:T(8,128)S(1)}, f32[16,8,512]{2,1,0:T(8,128)}, u32[]{:S(2)}) copy-start(f32[16,8,512]{2,1,0:T(8,128)} %param.15) | copy-start | bytes 786436
  6.5 0.9 %copy-start.8 = (f32[16,8,512]{2,1,0:T(8,128)S(1)}, f32[16,8,512]{2,1,0:T(8,128)}, u32[]{:S(2)}) copy-start(f32[16,8,512]{2,1,0:T(8,128)} %param.16) | copy-start | bytes 786436
  7.4 0.9 %copy-start.9 = (bf16[208,480]{1,0:T(8,128)(2,1)S(1)}, bf16[208,480]{1,0:T(8,128)(2,1)}, u32[]{:S(2)}) copy-start(bf16[208,480]{1,0:T(8,128)(2,1)} %constant.13.clone.gather_in) | copy-start | bytes 599044
  8.4 0.9 %copy-start.10 = (bf16[160,208]{1,0:T(8,128)(2,1)S(1)}, bf16[160,208]{1,0:T(8,128)(2,1)}, u32[]{:S(2)}) copy-start(bf16[160,208]{1,0:T(8,128)(2,1)} %constant.12.clone.pick_in) | copy-start | bytes 199684
  9.3 29.0 %copy-start.2 = (f32[16,8,512]{2,1,0:T(8,128)S(1)}, f32[16,8,512]{2,1,0:T(8,128)}, u32[]{:S(2)}) copy-start(f32[16,8,512]{2,1,0:T(8,128)} %param.17) | copy-start | bytes 786436
  9.3 29.0 %copy-start.3 = (f32[3,16,8,512]{3,2,1,0:T(8,128)S(1)}, f32[3,16,8,512]{3,2,1,0:T(8,128)}, u32[]{:S(2)}) copy-start(f32[3,16,8,512]{3,2,1,0:T(8,128)} %param.13) | copy-start | bytes 2359300
  9.3 29.0 %copy-start.4 = (f32[3,16,8,512]{3,2,1,0:T(8,128)S(1)}, f32[3,16,8,512]{3,2,1,0:T(8,128)}, u32[]{:S(2)}) copy-start(f32[3,16,8,512]{3,2,1,0:T(8,128)} %param.14) | copy-start | bytes 2359300
  9.3 29.1 %copy-start.11 = (f32[8,512]{1,0:T(8,128)S(1)}, f32[8,512]{1,0:T(8,128)}, u32[]{:S(2)}) copy-start(f32[8,512]{1,0:T(8,128)} %constant.14.clone.weight_zy) | copy-start | bytes 49156

commit v2 on v1

--- a/solution.py
+++ b/solution.py
@@ -103,37 +103,66 @@
     return jnp.dot(first, second, preferred_element_type=jnp.float32)
 
 
-def row_tables(nodes_x, nodes_z):
+def node_row(point, nodes_x, nodes_z):
+    own, elem_x, elem_z = nodes_x * nodes_z, nodes_x // 4, nodes_z // 4
+    tile = elem_x * elem_z
+    pair = point // tile
+    inside = point - pair * tile
+    a = (pair * 13) >> 6
+    b = pair - 5 * a
+    f = inside // elem_x
+    x = 4 * (inside - f * elem_x) + a
+    z = 4 * f + b
+    low = jnp.where(x < nodes_x, x * nodes_z + z, own + z)
+    high = own + nodes_z + jnp.where(x < nodes_x, x, nodes_x)
+    row = jnp.where(z < nodes_z, low, high)
+    return jnp.where(point < 25 * tile, row, -1)
+
+
+def selection(hits):
+    return jnp.where(hits, 1.0, 0.0).astype(jnp.bfloat16)
+
+
+def iotas(rows, columns):
+    return tuple(lax.broadcasted_iota(jnp.int32, (rows, columns), dim) for dim in range(2))
+
+
+def unfold_table(nodes_y):
+    node, place = iotas(nodes_y, nodes_y)
+    elem_y = nodes_y // 4
+    return selection(node == 4 * (place % elem_y) + place // elem_y)
+
+
+def fold_table(nodes_y):
+    elem_y = nodes_y // 4
+    place, node = iotas(5 * elem_y, nodes_y)
+    target = 4 * (place % elem_y) + place // elem_y
+    return selection(node == jnp.where(target >= nodes_y, target - nodes_y, target))
+
+
+def pick_table(nodes_x, nodes_z, points):
+    row, point = iotas(nodes_x * nodes_z + nodes_x + nodes_z + 8, points)
+    return selection(row == node_row(point, nodes_x, nodes_z))
+
+
+def own_table(nodes_x, nodes_z, points):
     own = nodes_x * nodes_z
-    elem_x, elem_z = nodes_x // 4, nodes_z // 4
-    tile = elem_x * elem_z
-    rows = own + nodes_z + nodes_x + 8
-    points = -(-25 * tile // 16) * 16
-    pick = np.zeros((points, rows), np.float32)
-    for a in range(5):
-        for b in range(5):
-            for f in range(elem_z):
-                for e in range(elem_x):
-                    x, z = 4 * e + a, 4 * f + b
-                    if x < nodes_x and z < nodes_z:
-                        row = x * nodes_z + z
-                    elif z < nodes_z:
-                        row = own + z
-                    elif x < nodes_x:
-                        row = own + nodes_z + x
-                    else:
-                        row = own + nodes_z + nodes_x
-                    pick[(a * 5 + b) * tile + f * elem_x + e, row] = 1.0
-    return pick
-
-
-def lane_tables(nodes_y):
-    elem_y = nodes_y // 4
-    fold = np.zeros((5 * elem_y, nodes_y), np.float32)
-    for c in range(5):
-        for g in range(elem_y):
-            fold[c * elem_y + g, (4 * g + c) % nodes_y] = 1.0
-    return fold
+    point, row = iotas(points, own)
+    hits = selection(row == node_row(point, nodes_x, nodes_z))
+    return jnp.concatenate([hits] * 3, axis=1)
+
+
+EDGE_BLOCKS = [(a, b) for a in range(5) for b in range(5) if a == 4 or b == 4]
+
+
+def edge_table(nodes_x, nodes_z):
+    own, edge, tile = nodes_x * nodes_z, nodes_x + nodes_z + 8, nodes_x * nodes_z // 16
+    place, column = iotas(len(EDGE_BLOCKS) * tile, 3 * edge)
+    block = place // tile
+    pair = jnp.where(block < 4, block * 5 + 4, block + 16)
+    row = node_row(pair * tile + place - block * tile, nodes_x, nodes_z) - own
+    inside = column % edge
+    return selection(inside == row)
 
 
 def step_kernel(
@@ -146,10 +175,6 @@
     shear,
     dense,
     kappa_in,
-    unfold_in,
-    fold_in,
-    pick_in,
-    gather_in,
     own_out,
     plane_in,
     level_in,
@@ -162,6 +187,7 @@
     pick,
     gather,
     lanes,
+    edge_lanes,
     views,
     grads,
     terms,
@@ -206,7 +232,6 @@
 
     loads = [(disp.at[i], fields.at[i, pl.ds(0, own)]) for i in range(3)]
     loads += [(ref, fields.at[3 + i, pl.ds(0, own)]) for i, ref in enumerate((lame, shear, dense))]
-    loads += [(unfold_in, unfold), (gather_in, gather), (pick_in, pick), (fold_in, fold)]
     loads += [(kappa_in, kappa)]
     loads = [
         pltpu.make_async_copy(source, target, load_sem.at[k])
@@ -219,6 +244,8 @@
     for k in range(1, rad):
         greet(column_peer(k))
     lax.fori_loop(1, surf, greet_line, 0)
+    unfold[...] = unfold_table(nodes_y)
+    gather[...] = own_table(nodes_x, nodes_z, points)
 
     for load in loads[:6]:
         load.wait()
@@ -248,30 +275,31 @@
     ]
     for copy in halos:
         copy.start()
+    for i in range(6):
+        split = jnp.concatenate(three_parts(fields[i, :own]), axis=0)
+        lanes[i] = dot(split, unfold[...]).astype(jnp.bfloat16)
+    for i in range(6):
+        views[i, :, :nodes_y] = dot(gather[...], lanes[i])
+    fold[...] = fold_table(nodes_y)
+    pick[...] = pick_table(nodes_x, nodes_z, points)
+    edge_gather = edge_table(nodes_x, nodes_z)
     for load in loads[6:]:
         load.wait()
-    for i in range(6):
-        split = jnp.concatenate(three_parts(fields[i, :own]), axis=0)
-        spread = dot(split, unfold[...]).astype(jnp.bfloat16)
-        for part in range(3):
-            lanes[i, part * rows_all : part * rows_all + own] = spread[part * own : (part + 1) * own]
     for copy in halos:
         copy.wait_recv()
     split = []
     for i in range(6):
         outer = jnp.where(r == rad - 1, 0.0, fields[i, own + nodes_z :])
         split += three_parts(jnp.concatenate([fields[i, own : own + nodes_z], outer], axis=0))
-    spread = dot(jnp.concatenate(split, axis=0), unfold[...]).astype(jnp.bfloat16)
+    edge_lanes[...] = dot(jnp.concatenate(split, axis=0), unfold[...]).astype(jnp.bfloat16)
     for i in range(6):
-        for part in range(3):
-            start = (3 * i + part) * edge_rows
-            lanes[i, part * rows_all + own : (part + 1) * rows_all] = spread[
-                start : start + edge_rows
+        start = 3 * i * edge_rows
+        added = dot(edge_gather, edge_lanes[start : start + 3 * edge_rows])
+        for k, (a, b) in enumerate(EDGE_BLOCKS):
+            views[i, (a * 5 + b) * tile : (a * 5 + b + 1) * tile, :nodes_y] += added[
+                k * tile : (k + 1) * tile
             ]
-    for i in range(6):
-        picked = dot(gather[...], lanes[i])
-        views[i, :, :nodes_y] = picked
-        views[i, :, nodes_y:] = pltpu.roll(picked[:, :elem_y], elem_y - 1, 1)
+        views[i, :, nodes_y:] = pltpu.roll(views[i, :, :elem_y], elem_y - 1, 1)
 
     def rows(a, b):
         return pl.ds(pl.multiple_of((a * 5 + b) * tile, tile), tile)
@@ -523,10 +551,8 @@
     own = nodes_x * nodes_z
     f32 = jnp.float32
     shape = jax.ShapeDtypeStruct
-    pick = row_tables(nodes_x, nodes_z)
-    fold = lane_tables(nodes_y)
-    points, rows = pick.shape
-    bf16 = functools.partial(jnp.asarray, dtype=jnp.bfloat16)
+    rows = own + nodes_z + nodes_x + 8
+    points = -(-25 * elem_x * elem_z // 16) * 16
     flat = functools.partial(jnp.reshape, shape=(3, own, nodes_y))
     flat_material = functools.partial(jnp.reshape, shape=(own, nodes_y))
     vmem = pltpu.VMEM
@@ -539,7 +565,7 @@
             shape((3, nodes_x + 8, nodes_y), f32),
             shape((elem_z, elem_x, elem_y), f32),
         ],
-        in_specs=[HBM] * 9,
+        in_specs=[HBM] * 5,
         out_specs=[VMEM] * 4,
         scratch_shapes=[
             vmem((6, rows, nodes_y), f32),
@@ -548,8 +574,9 @@
             vmem((nodes_y, nodes_y), jnp.bfloat16),
             vmem((5 * elem_y, nodes_y), jnp.bfloat16),
             vmem((rows, points), jnp.bfloat16),
-            vmem((points, 3 * rows), jnp.bfloat16),
-            vmem((6, 3 * rows, nodes_y), jnp.bfloat16),
+            vmem((points, 3 * own), jnp.bfloat16),
+            vmem((6, 3 * own, nodes_y), jnp.bfloat16),
+            vmem((18 * (rows - own), nodes_y), jnp.bfloat16),
             vmem((6, points, 5 * elem_y), f32),
             vmem((6, points, 5 * elem_y), f32),
             vmem((5, points, 5 * elem_y), f32),
@@ -558,7 +585,7 @@
             vmem((3, rows - own, nodes_y), f32),
             vmem((rad, elem_z + 1, surf, elem_x, elem_y), f32),
             vmem((rad * (elem_z + 1), surf * elem_x, elem_y), f32),
-            dma((11,)),
+            dma((7,)),
             dma((3,)),
             dma((3,)),
             dma((rad,)),
@@ -572,15 +599,16 @@
             collective_id=0, has_side_effects=True, vmem_limit_bytes=LIMIT
         ),
     )(
-        flat(displacement),
-        flat_material(lame_first),
-        flat_material(shear_modulus),
-        flat_material(density),
-        shell_kappa,
-        bf16(fold[:nodes_y].T),
-        bf16(fold),
-        bf16(pick.T),
-        bf16(np.concatenate([pick] * 3, axis=1)),
+        *[
+            pltpu.with_memory_space_constraint(operand, pltpu.HBM)
+            for operand in (
+                flat(displacement),
+                flat_material(lame_first),
+                flat_material(shear_modulus),
+                flat_material(density),
+                shell_kappa,
+            )
+        ]
     )
 
     line = np.array([2.0 * WEIGHTS[0], WEIGHTS[1], WEIGHTS[2], WEIGHTS[3]])

time: 40.3 us -> 32.4 us (0.80)
  local copies, waits for them, and re-layouts: 8.63 us -> 2.28 us
  Pallas kernels: 30.5 us -> 29.2 us
    unnamed x26 -> x10, local copies, waits for them, and re-layouts: 8.63 us -> 2.28 us
    pallas_call x1, Pallas kernels: 29 us -> 27.7 us  [on_device(): pl.pallas_call(functools.partial(step_kernel, surf, rad, nodes_x, nodes_z...]
where the time goes in v2:
time: 32.4 us; the launch traced here: 32.2 us
  Pallas kernels  29.2 us (90%)
  local copies, waits for them, and re-layouts  2.28 us (7%)
  between operations  0.7 us (2%)
    pallas_call x1, Pallas kernels, on_device(): pl.pallas_call(functools.partial(step_kernel, surf, rad, nodes_x, nodes_z...  27.7 us
    unnamed x10, local copies, waits for them, and re-layouts  2.28 us
    pallas_call x1, Pallas kernels, on_device(): pl.pallas_call(finish_kernel, out_shape=[shape((3, own, nodes_y), f32), s...  1.48 us

profile of v2, /device:TPU:0, one launch (start us, length us, event | category | flops | bytes accessed | tf_op | source)
XLA Modules:
  0.0 32.2 jit_solution(2310637640992152356)
XLA Ops:
  0.6 0.0 copy-start
  0.6 0.0 copy-start.1
  0.7 0.0 copy-start.4
  0.7 27.7 %shard_map.103 = (f32[3,128,512]{2,1,0:T(8,128)S(1)}, f32[3,8,512]{2,1,0:T(8,128)S(1)}, f32[3,24,512]{2,1,0:T(8,128)S(1)}, f32[2,4,128]{2,1,0:T(4,128)S(1)}) custom-call(f32[3,128,512]{2,1,0:T(8,128)} %bitcast.8, f32[128,512]{1,0:T(8,128)} %bitcast.14, f32[128,512]{1,0:T(8,128)} %bitcast.15, f32[128,512]{1,0:T(8,128)} %bitcast.10, f32[4,4,128]{2,1,0:T(4,128)} %kappa_in.1), custom_call_target="tpu_custom_call" | custom-call | tf_op jit(solution)/shard_map/pallas_call | solution.py:560
  28.4 0.0 copy-done
  28.4 0.0 copy-done.1
  28.4 0.0 copy-done.4
  28.4 0.0 copy-start.2
  28.4 1.1 %copy-done.2 = f32[3,16,8,512]{3,2,1,0:T(8,128)S(1)} copy-done((f32[3,16,8,512]{3,2,1,0:T(8,128)S(1)}, f32[3,16,8,512]{3,2,1,0:T(8,128)}, u32[]{:S(2)}) %copy-start.2) | copy-done | bytes 786456
  29.6 0.0 copy-start.3
  29.6 1.1 %copy-done.3 = f32[3,16,8,512]{3,2,1,0:T(8,128)S(1)} copy-done((f32[3,16,8,512]{3,2,1,0:T(8,128)S(1)}, f32[3,16,8,512]{3,2,1,0:T(8,128)}, u32[]{:S(2)}) %copy-start.3) | copy-done | bytes 786456
  30.7 1.5 %shard_map.104 = (f32[3,128,512]{2,1,0:T(8,128)}, f32[3,128,512]{2,1,0:T(8,128)}, f32[4,2,128]{2,1,0:T(2,128)}) custom-call(f32[3,128,512]{2,1,0:T(8,128)S(1)} %bitcast.9, f32[3,128,512]{2,1,0:T(8,128)S(1)} %bitcast.12, f32[3,128,512]{2,1,0:T(8,128)S(1)} %bitcast.13, f32[128,512]{1,0:T(8,128)S(1)} %bitcast.11, ...), custom_call_target="tpu_custom_call" | custom-call | tf_op jit(solution)/shard_map/pallas_call | solution.py:616
Async XLA Ops:
  0.6 27.8 %copy-start = (f32[3,16,8,512]{3,2,1,0:T(8,128)S(1)}, f32[3,16,8,512]{3,2,1,0:T(8,128)}, u32[]{:S(2)}) copy-start(f32[3,16,8,512]{3,2,1,0:T(8,128)} %param.8) | copy-start | bytes 2359300
  0.6 27.8 %copy-start.1 = (f32[16,8,512]{2,1,0:T(8,128)S(1)}, f32[16,8,512]{2,1,0:T(8,128)}, u32[]{:S(2)}) copy-start(f32[16,8,512]{2,1,0:T(8,128)} %param.13) | copy-start | bytes 786436
  0.7 27.8 %copy-start.4 = (f32[8,512]{1,0:T(8,128)S(1)}, f32[8,512]{1,0:T(8,128)}, u32[]{:S(2)}) copy-start(f32[8,512]{1,0:T(8,128)} %constant.2.clone.weight_zy) | copy-start | bytes 49156
  28.4 1.1 %copy-start.2 = (f32[3,16,8,512]{3,2,1,0:T(8,128)S(1)}, f32[3,16,8,512]{3,2,1,0:T(8,128)}, u32[]{:S(2)}) copy-start(f32[3,16,8,512]{3,2,1,0:T(8,128)} %param.9) | copy-start | bytes 2359300
  29.6 1.1 %copy-start.3 = (f32[3,16,8,512]{3,2,1,0:T(8,128)S(1)}, f32[3,16,8,512]{3,2,1,0:T(8,128)}, u32[]{:S(2)}) copy-start(f32[3,16,8,512]{3,2,1,0:T(8,128)} %param.10) | copy-start | bytes 2359300
